TPU v7x, 512 devices: a whole 4x8x8 slice. The times are simulated.
512 devices in a mesh: wide: 64 (over y, x, z_lo), narrow: 8 (over z_hi, core).
Axes of the slice: x: 4, y: 8, z: 8 (z_hi: 4, z_lo: 2; z = z_hi * 2 + z_lo), core: 2. Of those that a mesh axis runs over, the one named last changes fastest.
Arguments:
- tval: bfloat16 [4096, 12, 128, 128], P(('wide', 'narrow')), may hold values from -0.16992188 to 0.16992188
- tcol: int32 [4096, 12], replicated, may hold values from 0 to 4095, as said below
- ocol: int32 [4096, 12], P(('wide', 'narrow')), may hold values from 0 to 4095, as said below
- basis: bfloat16 [524288, 128], P(('wide', 'narrow')), may hold values from -6 to 6
Outputs:
- projected: bfloat16 [524288, 128], P(('wide', 'narrow'))
- level: float32 [128, 128], replicated
Inputs may be any that keep to these rules, and one draw needn't show every extreme that they name: `tcol`: the 12 block columns of row i are distinct, include i, and each lies within cyclic distance 8 of i modulo 4096. `ocol`: the 12 block columns of row i are distinct, include i, and each lies within cyclic distance 8 of i modulo 4096.
All inputs are finite; a program needn't handle non-finite values.
Results may differ from a plain program's by a relative error of at most 0.0049.
Values may be sent and summed in bfloat16 or wider, within the bound.
No kernel may reach another device: no remote copies, remote signals or barrier semaphores. Data moves between devices by JAX's collectives and lax.ppermute only.
A program may use at most 64 MiB of HBM per device.

v0:
```python
import jax
import jax.numpy as jnp
from jax import lax
from jax.sharding import PartitionSpec as P


def with_halo(cells, sides, width):
    for axis, dim in sides:
        count = lax.axis_size(axis)
        head = lax.slice_in_dim(cells, 0, width, axis=dim)
        tail = lax.slice_in_dim(cells, cells.shape[dim] - width, cells.shape[dim], axis=dim)
        cells = jnp.concatenate(
            [
                lax.ppermute(tail, axis, [(i, (i + 1) % count) for i in range(count)]),
                cells,
                lax.ppermute(head, axis, [((i + 1) % count, i) for i in range(count)]),
            ],
            axis=dim,
        )
    return cells


def per_device(tval, tcol, ocol, basis):
    local = tval.shape[0]
    size = tval.shape[2]
    width = basis.shape[1]
    slots = tval.shape[1]
    devices = lax.axis_size(("wide", "narrow"))
    count = local * devices
    first = lax.axis_index(("wide", "narrow")) * local
    extended = with_halo(tval, ((("wide", "narrow"), 0),), local)
    basis_ext = with_halo(basis, ((("wide", "narrow"), 0),), local * size)
    basis_blocks = basis_ext.reshape(3 * local, size, width)
    slot_ids = jnp.arange(slots, dtype=jnp.int32)

    def one_row(index):
        glob = first + index
        cols = tcol[glob]
        places = (cols - first + local) % count
        pattern = tcol[cols]
        outcols = ocol[index]
        match = (pattern[None, :, :] == outcols[:, None, None]).astype(jnp.int32)
        which = jnp.sum(match * slot_ids[None, None, :], axis=2)
        valid = jnp.sum(match, axis=2).astype(jnp.bfloat16)
        chosen = extended[places[None, :], which]
        selected = chosen * valid[:, :, None, None]
        square = jnp.einsum(
            "sab,osbc->oac", tval[index], selected, preferred_element_type=jnp.float32
        ).astype(jnp.bfloat16)
        picked = basis_blocks[(outcols - first + local) % count]
        result = jnp.einsum("oac,ock->ak", square, picked, preferred_element_type=jnp.float32)
        return result.astype(jnp.bfloat16)

    projected = lax.map(one_row, jnp.arange(local, dtype=jnp.int32)).reshape(local * size, width)
    partial_level = jnp.dot(basis.T, projected, preferred_element_type=jnp.float32)
    level = lax.psum(partial_level, ("wide", "narrow"))
    level = level / jnp.sqrt(jnp.float32(count * size))
    return (projected, level)


def solution(mesh):
    return jax.shard_map(
        per_device,
        mesh=mesh,
        in_specs=(
            P(("wide", "narrow"), None, None, None),
            P(),
            P(("wide", "narrow"), None),
            P(("wide", "narrow"), None),
        ),
        out_specs=(P(("wide", "narrow"), None), P()),
        check_vma=False,
    )
```

profile of v0, /device:TPU:1, one launch (start us, length us, event | category | flops | bytes accessed | tf_op | source)
XLA Modules:
  0.0 650.9 jit_solution(2711179265260050932)
XLA Ops:
  7.2 7.2 %collective-permute-start = (bf16[8,12,128,128]{3,2,1,0:T(8,128)(2,1)}, bf16[8,12,128,128]{3,2,1,0:T(8,128)(2,1)}, u32[]{:S(2)}, u32[]{:S(2)}) collective-permute-start(bf16[8,12,128,128]{3,2,1,0:T(8,128)(2,1)} %param.6), channel_id=1, source_target_pairs={{0,1},{1,2},{2,3},{3,4},{4,5},{5,6},{6,7},{7,8},{8,9},{9,10},{10,1... | collective-permute-start | bytes 9437192 | tf_op jit(solution)/shard_map/ppermute | solution.py:14
  20.9 9.1 %collective-permute-start.3 = (bf16[1024,128]{1,0:T(8,128)(2,1)}, bf16[1024,128]{1,0:T(8,128)(2,1)S(1)}, u32[]{:S(2)}, u32[]{:S(2)}) collective-permute-start(bf16[1024,128]{1,0:T(8,128)(2,1)} %param.9), channel_id=1, source_target_pairs={{1,0},{2,1},{3,2},{4,3},{5,4},{6,5},{7,6},{8,7},{9,8},{10,9},{11,1... | collective-permute-start | bytes 786440 | tf_op jit(solution)/shard_map/ppermute | solution.py:16
  31.6 55.9 %collective-permute-done.2 = bf16[1024,128]{1,0:T(8,128)(2,1)S(1)} collective-permute-done((bf16[1024,128]{1,0:T(8,128)(2,1)}, bf16[1024,128]{1,0:T(8,128)(2,1)S(1)}, u32[]{:S(2)}, u32[]{:S(2)}) %collective-permute-start.2) | collective-permute-done | bytes 262176 | tf_op jit(solution)/shard_map/ppermute | solution.py:14
  87.5 6.0 collective-permute-done.3
  94.5 7.7 %pad_maximum_fusion = bf16[24,12,128,128]{3,2,1,0:T(8,128)(2,1)} fusion(bf16[8,12,128,128]{3,2,1,0:T(8,128)(2,1)} %collective-permute-done.1, bf16[8,12,128,128]{3,2,1,0:T(8,128)(2,1)} %param.6, bf16[8,12,128,128]{3,2,1,0:T(8,128)(2,1)} %collective-permute-done), kind=kLoop, calls=%fused_computation.47 | loop fusion | flops 9437184 | bytes 18874368 | tf_op jit(solution)/shard_map/concatenate | solution.py:12
  102.2 269.6 %while.13 = (s32[]{:T(128)}, bf16[8,128,128]{2,1,0:T(8,128)(2,1)}, s32[8]{0:T(128)S(1)}, s32[]{:T(128)}, s32[4096,12]{1,0:T(8,128)S(1)}, /*index=5*/s32[8,12]{1,...) while((s32[]{:T(128)}, bf16[8,128,128]{2,1,0:T(8,128)(2,1)}, ...), condition=%wide.region_3.4_spmd.clone, body=%wide.region_0.3_spmd.clone.sunk | while | flops 656895552 | bytes 25215700 | solution.py:54
  108.0 15.8 %gather_fusion.2 = bf16[144,128,128]{2,1,0:T(8,128)(2,1)} fusion(bf16[24,12,128,128]{3,2,1,0:T(8,128)(2,1)} %get-tuple-element.305, s32[144]{0:T(256)S(1)} %reshape.191), kind=kCustom, calls=%fused_computation.1.clone.clone.1 | custom fusion | bytes 9438336 | tf_op jit(solution)/shard_map/while/body/eval_jaxpr/gather | solution.py:45
  123.8 6.7 %copy.17 = bf16[12,12,128,128]{2,3,1,0:T(8,128)(2,1)} copy(bf16[12,12,128,128]{3,2,1,0:T(8,128)(2,1)} %bitcast.95) | data formatting | bytes 9437184 | tf_op jit(solution)/shard_map/while/body/eval_jaxpr/gather | solution.py:45
  141.7 15.8 %gather_fusion.2 = bf16[144,128,128]{2,1,0:T(8,128)(2,1)} fusion(bf16[24,12,128,128]{3,2,1,0:T(8,128)(2,1)} %get-tuple-element.305, s32[144]{0:T(256)S(1)} %reshape.191), kind=kCustom, calls=%fused_computation.1.clone.clone.1 | custom fusion | bytes 9438336 | tf_op jit(solution)/shard_map/while/body/eval_jaxpr/gather | solution.py:45
  157.5 6.7 %copy.17 = bf16[12,12,128,128]{2,3,1,0:T(8,128)(2,1)} copy(bf16[12,12,128,128]{3,2,1,0:T(8,128)(2,1)} %bitcast.95) | data formatting | bytes 9437184 | tf_op jit(solution)/shard_map/while/body/eval_jaxpr/gather | solution.py:45
  175.4 15.8 %gather_fusion.2 = bf16[144,128,128]{2,1,0:T(8,128)(2,1)} fusion(bf16[24,12,128,128]{3,2,1,0:T(8,128)(2,1)} %get-tuple-element.305, s32[144]{0:T(256)S(1)} %reshape.191), kind=kCustom, calls=%fused_computation.1.clone.clone.1 | custom fusion | bytes 9438336 | tf_op jit(solution)/shard_map/while/body/eval_jaxpr/gather | solution.py:45
  191.2 6.7 %copy.17 = bf16[12,12,128,128]{2,3,1,0:T(8,128)(2,1)} copy(bf16[12,12,128,128]{3,2,1,0:T(8,128)(2,1)} %bitcast.95) | data formatting | bytes 9437184 | tf_op jit(solution)/shard_map/while/body/eval_jaxpr/gather | solution.py:45
  209.1 15.8 %gather_fusion.2 = bf16[144,128,128]{2,1,0:T(8,128)(2,1)} fusion(bf16[24,12,128,128]{3,2,1,0:T(8,128)(2,1)} %get-tuple-element.305, s32[144]{0:T(256)S(1)} %reshape.191), kind=kCustom, calls=%fused_computation.1.clone.clone.1 | custom fusion | bytes 9438336 | tf_op jit(solution)/shard_map/while/body/eval_jaxpr/gather | solution.py:45
  224.9 6.7 %copy.17 = bf16[12,12,128,128]{2,3,1,0:T(8,128)(2,1)} copy(bf16[12,12,128,128]{3,2,1,0:T(8,128)(2,1)} %bitcast.95) | data formatting | bytes 9437184 | tf_op jit(solution)/shard_map/while/body/eval_jaxpr/gather | solution.py:45
  242.8 15.8 %gather_fusion.2 = bf16[144,128,128]{2,1,0:T(8,128)(2,1)} fusion(bf16[24,12,128,128]{3,2,1,0:T(8,128)(2,1)} %get-tuple-element.305, s32[144]{0:T(256)S(1)} %reshape.191), kind=kCustom, calls=%fused_computation.1.clone.clone.1 | custom fusion | bytes 9438336 | tf_op jit(solution)/shard_map/while/body/eval_jaxpr/gather | solution.py:45
  258.6 6.7 %copy.17 = bf16[12,12,128,128]{2,3,1,0:T(8,128)(2,1)} copy(bf16[12,12,128,128]{3,2,1,0:T(8,128)(2,1)} %bitcast.95) | data formatting | bytes 9437184 | tf_op jit(solution)/shard_map/while/body/eval_jaxpr/gather | solution.py:45
  276.5 15.8 %gather_fusion.2 = bf16[144,128,128]{2,1,0:T(8,128)(2,1)} fusion(bf16[24,12,128,128]{3,2,1,0:T(8,128)(2,1)} %get-tuple-element.305, s32[144]{0:T(256)S(1)} %reshape.191), kind=kCustom, calls=%fused_computation.1.clone.clone.1 | custom fusion | bytes 9438336 | tf_op jit(solution)/shard_map/while/body/eval_jaxpr/gather | solution.py:45
  292.3 6.7 %copy.17 = bf16[12,12,128,128]{2,3,1,0:T(8,128)(2,1)} copy(bf16[12,12,128,128]{3,2,1,0:T(8,128)(2,1)} %bitcast.95) | data formatting | bytes 9437184 | tf_op jit(solution)/shard_map/while/body/eval_jaxpr/gather | solution.py:45
  299.7 4.8 fusion.66
  310.2 15.8 %gather_fusion.2 = bf16[144,128,128]{2,1,0:T(8,128)(2,1)} fusion(bf16[24,12,128,128]{3,2,1,0:T(8,128)(2,1)} %get-tuple-element.305, s32[144]{0:T(256)S(1)} %reshape.191), kind=kCustom, calls=%fused_computation.1.clone.clone.1 | custom fusion | bytes 9438336 | tf_op jit(solution)/shard_map/while/body/eval_jaxpr/gather | solution.py:45
  326.1 6.7 %copy.17 = bf16[12,12,128,128]{2,3,1,0:T(8,128)(2,1)} copy(bf16[12,12,128,128]{3,2,1,0:T(8,128)(2,1)} %bitcast.95) | data formatting | bytes 9437184 | tf_op jit(solution)/shard_map/while/body/eval_jaxpr/gather | solution.py:45
  343.9 15.8 %gather_fusion.2 = bf16[144,128,128]{2,1,0:T(8,128)(2,1)} fusion(bf16[24,12,128,128]{3,2,1,0:T(8,128)(2,1)} %get-tuple-element.305, s32[144]{0:T(256)S(1)} %reshape.191), kind=kCustom, calls=%fused_computation.1.clone.clone.1 | custom fusion | bytes 9438336 | tf_op jit(solution)/shard_map/while/body/eval_jaxpr/gather | solution.py:45
  359.8 6.7 %copy.17 = bf16[12,12,128,128]{2,3,1,0:T(8,128)(2,1)} copy(bf16[12,12,128,128]{3,2,1,0:T(8,128)(2,1)} %bitcast.95) | data formatting | bytes 9437184 | tf_op jit(solution)/shard_map/while/body/eval_jaxpr/gather | solution.py:45
  373.7 268.7 %all-reduce.2.cloned.1.call-done = f32[128,128]{0,1:T(8,128)} async-done(((f32[128,128]{0,1:T(8,128)}), f32[128,128]{0,1:T(8,128)}) %all-reduce.2.cloned.1.call-update) | async-done | bytes 65552 | tf_op jit(solution)/shard_map/psum | solution.py:56
  (110 shorter events, 77.0 us)
Async XLA Ops:
  7.2 635.3 %all-reduce.2.cloned.1.call-start = ((), (), s32[]{:S(2)}) async-start(), calls=%async_computation | async-start | bytes 131072 | tf_op jit(solution)/shard_map/psum | solution.py:56
  7.2 87.3 %collective-permute-start = (bf16[8,12,128,128]{3,2,1,0:T(8,128)(2,1)}, bf16[8,12,128,128]{3,2,1,0:T(8,128)(2,1)}, u32[]{:S(2)}, u32[]{:S(2)}) collective-permute-start(bf16[8,12,128,128]{3,2,1,0:T(8,128)(2,1)} %param.6), channel_id=1, source_target_pairs={{0,1},{1,2},{2,3},{3,4},{4,5},{5,6},{6,7},{7,8},{8,9},{9,10},{10,1... | collective-permute-start | bytes 9437192 | tf_op jit(solution)/shard_map/ppermute | solution.py:14
  14.4 80.1 %collective-permute-start.1 = (bf16[8,12,128,128]{3,2,1,0:T(8,128)(2,1)}, bf16[8,12,128,128]{3,2,1,0:T(8,128)(2,1)}, u32[]{:S(2)}, u32[]{:S(2)}) collective-permute-start(bf16[8,12,128,128]{3,2,1,0:T(8,128)(2,1)} %param.6), channel_id=1, source_target_pairs={{1,0},{2,1},{3,2},{4,3},{5,4},{6,5},{7,6},{8,7},{9,8},{10,9},{11,1... | collective-permute-start | bytes 9437192 | tf_op jit(solution)/shard_map/ppermute | solution.py:16
  17.9 69.6 %collective-permute-start.2 = (bf16[1024,128]{1,0:T(8,128)(2,1)}, bf16[1024,128]{1,0:T(8,128)(2,1)S(1)}, u32[]{:S(2)}, u32[]{:S(2)}) collective-permute-start(bf16[1024,128]{1,0:T(8,128)(2,1)} %param.9), channel_id=1, source_target_pairs={{0,1},{1,2},{2,3},{3,4},{4,5},{5,6},{6,7},{7,8},{8,9},{9,10},{10,1... | collective-permute-start | bytes 786440 | tf_op jit(solution)/shard_map/ppermute | solution.py:14
  20.9 72.6 %collective-permute-start.3 = (bf16[1024,128]{1,0:T(8,128)(2,1)}, bf16[1024,128]{1,0:T(8,128)(2,1)S(1)}, u32[]{:S(2)}, u32[]{:S(2)}) collective-permute-start(bf16[1024,128]{1,0:T(8,128)(2,1)} %param.9), channel_id=1, source_target_pairs={{1,0},{2,1},{3,2},{4,3},{5,4},{6,5},{7,6},{8,7},{9,8},{10,9},{11,1... | collective-permute-start | bytes 786440 | tf_op jit(solution)/shard_map/ppermute | solution.py:16
  102.2 269.6 %copy-start = (bf16[1024,128]{1,0:T(8,128)(2,1)S(1)}, bf16[1024,128]{1,0:T(8,128)(2,1)}, u32[]{:S(2)}) copy-start(bf16[1024,128]{1,0:T(8,128)(2,1)} %param.9) | copy-start | bytes 786436
Sparse Core Ops, SparseCore 0:
  373.8 268.5 all-reduce.1
where the time goes:
time: 653 us; the launch traced here: 651 us
  waiting for transfers between devices  331 us (51%)
  local copies, waits for them, and re-layouts  197 us (30%)
  matrix products  40 us (6%)
  other arithmetic  25.5 us (4%)
  starting transfers between devices  22.8 us (3%)
  loops' own time  20.3 us (3%)
  between operations  14.1 us (2%)
    psum x1, waiting for transfers between devices, per_device(): level = lax.psum(partial_level, ('wide', 'narrow'))  269 us
    gather x16, local copies, waits for them, and re-layouts, one_row(): chosen = extended[places[None, :], which]  180 us
    ppermute x2, waiting for transfers between devices, with_halo(): lax.ppermute(tail, axis, [(i, (i + 1) % count) for i in range(count)])  55.9 us
    dot_general x8, matrix products, one_row(): jnp.einsum('oac,ock->ak', square, picked, preferred_element_type=jnp.floa...  38.2 us
    another operation x1, loops' own time, per_device(): lax.map(one_row, jnp.arange(local, dtype=jnp.int32))  20.3 us
  transfers between devices with their start and end apart: 5, of which 3 were waited for; matrix products, arithmetic and copies ran while one was open for 0% of the time, Pallas kernels for 0%

commit v1 on v0

--- a/solution.py
+++ b/solution.py
@@ -53,7 +53,7 @@
 
     projected = lax.map(one_row, jnp.arange(local, dtype=jnp.int32)).reshape(local * size, width)
     partial_level = jnp.dot(basis.T, projected, preferred_element_type=jnp.float32)
-    level = lax.psum(partial_level, ("wide", "narrow"))
+    level = jnp.sum(lax.all_gather(partial_level, ("wide", "narrow")), axis=0)
     level = level / jnp.sqrt(jnp.float32(count * size))
     return (projected, level)
 

time: 653 us -> 1290 us (1.98)
  waiting for transfers between devices: 331 us -> 949 us
  local copies, waits for them, and re-layouts: 197 us -> 215 us
    all_gather x0 -> x1, waiting for transfers between devices: none -> 891 us  [per_device(): level = jnp.sum(lax.all_gather(partial_level, ('wide', 'narrow')), axis=0)]
    psum x1 -> x0, waiting for transfers between devices: 269 us -> none  [per_device(): level = lax.psum(partial_level, ('wide', 'narrow'))]
    ppermute x2, waiting for transfers between devices: 55.9 us -> 0.01 us  [with_halo(): lax.ppermute(tail, axis, [(i, (i + 1) % count) for i in range(count)])]
    ppermute x2, waiting for transfers between devices: 6 us -> 57.3 us  [with_halo(): lax.ppermute(head, axis, [((i + 1) % count, i) for i in range(count)])]
    unnamed x4 -> x5, local copies, waits for them, and re-layouts: 2.3 us -> 19.5 us
  transfers between devices with their start and end apart: 5 -> 5, of which waited for: 3 -> 2; matrix products, arithmetic and copies ran while one was open for 0% -> 0% of each run, Pallas kernels for 0% -> 0%
where the time goes in v1:
time: 1290 us
  waiting for transfers between devices  949 us (74%)
  local copies, waits for them, and re-layouts  215 us (17%)
  matrix products  40.1 us (3%)
  other arithmetic  28.6 us (2%)
  starting transfers between devices  22.8 us (2%)
  loops' own time  20.4 us (2%)
  between operations  14.1 us (1%)
    all_gather x1, waiting for transfers between devices, per_device(): level = jnp.sum(lax.all_gather(partial_level, ('wide', 'narrow')), axis=0)  891 us
    gather x16, local copies, waits for them, and re-layouts, one_row(): chosen = extended[places[None, :], which]  180 us
    ppermute x2, waiting for transfers between devices, with_halo(): lax.ppermute(head, axis, [((i + 1) % count, i) for i in range(count)])  57.3 us
    dot_general x8, matrix products, one_row(): jnp.einsum('oac,ock->ak', square, picked, preferred_element_type=jnp.floa...  38.2 us
  transfers between devices with their start and end apart: 5, of which 2 were waited for; matrix products, arithmetic and copies ran while one was open for 0% of the time, Pallas kernels for 0%

profile of v1, /device:TPU:1, one launch (start us, length us, event | category | flops | bytes accessed | tf_op | source)
XLA Modules:
  0.0 1289.4 jit_solution(3569394387608713950)
XLA Ops:
  7.2 8.8 collective-permute-start.1
  17.9 10.1 collective-permute-start.3
  31.6 57.3 %collective-permute-done.3 = bf16[1024,128]{1,0:T(8,128)(2,1)S(1)} collective-permute-done((bf16[1024,128]{1,0:T(8,128)(2,1)}, bf16[1024,128]{1,0:T(8,128)(2,1)S(1)}, u32[]{:S(2)}, u32[]{:S(2)}) %collective-permute-start.3) | collective-permute-done | bytes 262176 | tf_op jit(solution)/shard_map/ppermute | solution.py:16
  90.0 7.7 pad_maximum_fusion
  97.7 269.7 %while.13 = (s32[]{:T(128)}, bf16[8,128,128]{2,1,0:T(8,128)(2,1)}, s32[8]{0:T(128)S(1)}, s32[]{:T(128)}, s32[4096,12]{1,0:T(8,128)S(1)}, /*index=5*/s32[8,12]{1,...) while((s32[]{:T(128)}, bf16[8,128,128]{2,1,0:T(8,128)(2,1)}, ...), condition=%wide.region_3.4_spmd.clone, body=%wide.region_0.3_spmd.clone.sunk | while | flops 656895552 | bytes 25215200 | solution.py:54
  104.1 15.8 %gather_fusion.2 = bf16[144,128,128]{2,1,0:T(8,128)(2,1)} fusion(bf16[24,12,128,128]{3,2,1,0:T(8,128)(2,1)} %get-tuple-element.312, s32[144]{0:T(256)S(1)} %reshape.192), kind=kCustom, calls=%fused_computation.1.clone.clone.1 | custom fusion | bytes 9438336 | tf_op jit(solution)/shard_map/while/body/eval_jaxpr/gather | solution.py:45
  119.9 6.7 copy.20
  126.6 4.8 fusion.66
  137.8 15.8 %gather_fusion.2 = bf16[144,128,128]{2,1,0:T(8,128)(2,1)} fusion(bf16[24,12,128,128]{3,2,1,0:T(8,128)(2,1)} %get-tuple-element.312, s32[144]{0:T(256)S(1)} %reshape.192), kind=kCustom, calls=%fused_computation.1.clone.clone.1 | custom fusion | bytes 9438336 | tf_op jit(solution)/shard_map/while/body/eval_jaxpr/gather | solution.py:45
  153.6 6.7 copy.20
  171.5 15.8 %gather_fusion.2 = bf16[144,128,128]{2,1,0:T(8,128)(2,1)} fusion(bf16[24,12,128,128]{3,2,1,0:T(8,128)(2,1)} %get-tuple-element.312, s32[144]{0:T(256)S(1)} %reshape.192), kind=kCustom, calls=%fused_computation.1.clone.clone.1 | custom fusion | bytes 9438336 | tf_op jit(solution)/shard_map/while/body/eval_jaxpr/gather | solution.py:45
  187.3 6.7 copy.20
  205.2 15.8 %gather_fusion.2 = bf16[144,128,128]{2,1,0:T(8,128)(2,1)} fusion(bf16[24,12,128,128]{3,2,1,0:T(8,128)(2,1)} %get-tuple-element.312, s32[144]{0:T(256)S(1)} %reshape.192), kind=kCustom, calls=%fused_computation.1.clone.clone.1 | custom fusion | bytes 9438336 | tf_op jit(solution)/shard_map/while/body/eval_jaxpr/gather | solution.py:45
  221.1 6.7 copy.20
  238.9 15.8 %gather_fusion.2 = bf16[144,128,128]{2,1,0:T(8,128)(2,1)} fusion(bf16[24,12,128,128]{3,2,1,0:T(8,128)(2,1)} %get-tuple-element.312, s32[144]{0:T(256)S(1)} %reshape.192), kind=kCustom, calls=%fused_computation.1.clone.clone.1 | custom fusion | bytes 9438336 | tf_op jit(solution)/shard_map/while/body/eval_jaxpr/gather | solution.py:45
  254.8 6.7 copy.20
  272.6 15.8 %gather_fusion.2 = bf16[144,128,128]{2,1,0:T(8,128)(2,1)} fusion(bf16[24,12,128,128]{3,2,1,0:T(8,128)(2,1)} %get-tuple-element.312, s32[144]{0:T(256)S(1)} %reshape.192), kind=kCustom, calls=%fused_computation.1.clone.clone.1 | custom fusion | bytes 9438336 | tf_op jit(solution)/shard_map/while/body/eval_jaxpr/gather | solution.py:45
  288.5 6.7 copy.20
  306.4 15.8 %gather_fusion.2 = bf16[144,128,128]{2,1,0:T(8,128)(2,1)} fusion(bf16[24,12,128,128]{3,2,1,0:T(8,128)(2,1)} %get-tuple-element.312, s32[144]{0:T(256)S(1)} %reshape.192), kind=kCustom, calls=%fused_computation.1.clone.clone.1 | custom fusion | bytes 9438336 | tf_op jit(solution)/shard_map/while/body/eval_jaxpr/gather | solution.py:45
  322.2 6.7 copy.20
  340.1 15.8 %gather_fusion.2 = bf16[144,128,128]{2,1,0:T(8,128)(2,1)} fusion(bf16[24,12,128,128]{3,2,1,0:T(8,128)(2,1)} %get-tuple-element.312, s32[144]{0:T(256)S(1)} %reshape.192), kind=kCustom, calls=%fused_computation.1.clone.clone.1 | custom fusion | bytes 9438336 | tf_op jit(solution)/shard_map/while/body/eval_jaxpr/gather | solution.py:45
  355.9 6.7 copy.20
  369.3 891.3 %all-gather.3.cloned.1.call-done = f32[65536,128]{0,1:T(8,128)} async-done(((f32[128,128]{0,1:T(8,128)}), f32[65536,128]{0,1:T(8,128)}) %all-gather.3.cloned.1.call-update) | async-done | bytes 33554448 | tf_op jit(solution)/shard_map/all_gather | solution.py:56
  1260.6 17.2 %copy.18 = f32[16,8,512,128]{3,2,1,0:T(8,128)S(1)} copy(f32[16,8,512,128]{3,1,2,0:T(8,128)} %bitcast.101) | data formatting | bytes 67108864
  (112 shorter events, 77.6 us)
Async XLA Ops:
  7.2 1253.4 %all-gather.3.cloned.1.call-start = ((), (), s32[]{:S(2)}) async-start(), calls=%async_computation | async-start | bytes 33619968 | tf_op jit(solution)/shard_map/all_gather | solution.py:56
  7.2 82.7 %collective-permute-start.1 = (bf16[8,12,128,128]{3,2,1,0:T(8,128)(2,1)}, bf16[8,12,128,128]{3,2,1,0:T(8,128)(2,1)}, u32[]{:S(2)}, u32[]{:S(2)}) collective-permute-start(bf16[8,12,128,128]{3,2,1,0:T(8,128)(2,1)} %param.6), channel_id=1, source_target_pairs={{1,0},{2,1},{3,2},{4,3},{5,4},{6,5},{7,6},{8,7},{9,8},{10,9},{11,1... | collective-permute-start | bytes 9437192 | tf_op jit(solution)/shard_map/ppermute | solution.py:16
  16.0 73.9 %collective-permute-start = (bf16[8,12,128,128]{3,2,1,0:T(8,128)(2,1)}, bf16[8,12,128,128]{3,2,1,0:T(8,128)(2,1)}, u32[]{:S(2)}, u32[]{:S(2)}) collective-permute-start(bf16[8,12,128,128]{3,2,1,0:T(8,128)(2,1)} %param.6), channel_id=1, source_target_pairs={{0,1},{1,2},{2,3},{3,4},{4,5},{5,6},{6,7},{7,8},{8,9},{9,10},{10,1... | collective-permute-start | bytes 9437192 | tf_op jit(solution)/shard_map/ppermute | solution.py:14
  17.9 71.0 %collective-permute-start.3 = (bf16[1024,128]{1,0:T(8,128)(2,1)}, bf16[1024,128]{1,0:T(8,128)(2,1)S(1)}, u32[]{:S(2)}, u32[]{:S(2)}) collective-permute-start(bf16[1024,128]{1,0:T(8,128)(2,1)} %param.9), channel_id=1, source_target_pairs={{1,0},{2,1},{3,2},{4,3},{5,4},{6,5},{7,6},{8,7},{9,8},{10,9},{11,1... | collective-permute-start | bytes 786440 | tf_op jit(solution)/shard_map/ppermute | solution.py:16
  28.1 60.9 %collective-permute-start.2 = (bf16[1024,128]{1,0:T(8,128)(2,1)}, bf16[1024,128]{1,0:T(8,128)(2,1)S(1)}, u32[]{:S(2)}, u32[]{:S(2)}) collective-permute-start(bf16[1024,128]{1,0:T(8,128)(2,1)} %param.9), channel_id=1, source_target_pairs={{0,1},{1,2},{2,3},{3,4},{4,5},{5,6},{6,7},{7,8},{8,9},{9,10},{10,1... | collective-permute-start | bytes 786440 | tf_op jit(solution)/shard_map/ppermute | solution.py:14
  97.7 269.7 %copy-start = (bf16[1024,128]{1,0:T(8,128)(2,1)S(1)}, bf16[1024,128]{1,0:T(8,128)(2,1)}, u32[]{:S(2)}) copy-start(bf16[1024,128]{1,0:T(8,128)(2,1)} %param.9) | copy-start | bytes 786436
Sparse Core Ops, SparseCore 0:
  369.4 891.1 all-gather.2
